TPU v7x, 256 devices: a whole 4x4x8 slice. The times are simulated.
256 devices in a mesh: dom: 256 (over z, x, y, core).
Axes of the slice: x: 4, y: 4, z: 8, core: 2. Of those that a mesh axis runs over, the one named last changes fastest.
Arguments:
- coef_init: float32 [1024, 128], P('dom'), may hold values from -6 to 6
- basis: bfloat16 [393216, 1024], P('dom'), may hold values from -0.75 to 0.75
- basis_scale: float32 [3072], P('dom'), may hold values from 0.5 to 2
- ext_force: float32 [393216, 128], P('dom'), may hold values from -6 to 6
- precond: float32 [1024], P('dom'), may hold values from 0.5 to 6, as said below
- connectivity: int32 [115200, 8], P('dom'), may hold values from 0 to 767, as said below
- halo_nodes: int32 [65536], P('dom'), may hold values from 0 to 511, as said below
- plastic: int32 [115200], P('dom'), may hold values 0 or 1
Outputs:
- coef_final: float32 [1024, 128], P('dom')
- nodal_residual: float32 [393216, 128], P('dom')
Inputs may be any that keep to these rules, and one draw needn't show every extreme that they name: `connectivity`: each part is a structured block of 16 x 16 x 2 nodes, numbered in a part-specific order; each row lists an element's 8 corners in corner-bit order (bit 0 along x, bit 1 along y, bit 2 along z). Entries below 512 are the part's own nodes; an entry 512 + h names the node listed h-th in the next part's halo_nodes (the next part's first z layer). `halo_nodes`: the entries of one part are its own local node numbers of its first z layer, in grid order with x fastest, all distinct. `precond`: Positive.
All inputs are finite; a program needn't handle non-finite values. No bound on the sum of `plastic` on one device may be relied on, other than what follows from the above.
Results may differ from a plain program's by a relative error of at most 0.0087.
Values may be sent and summed in bfloat16 or wider, within the bound.
A program may use at most 64 MiB of HBM per device.

v0:
```python
import jax
import jax.numpy as jnp
from jax import lax
from jax.sharding import PartitionSpec as P

R = 1024
ITERS = 2


STEP_SIZE = 0.5
SHEAR_MODULUS = 1.0
LAME_FIRST = 1.5
HARDENING = 0.5
YIELD_STRESS = 3.0
EPSILON = 1e-05


def from_behind(value, axis, steps):
    count = lax.axis_size(axis)
    leading, last = (max(0, -steps), min(count, count - steps))
    return lax.ppermute(value, axis, [(source, source + steps) for source in range(leading, last)])


def corner_table():
    corner_bits = jnp.arange(8)[:, None] >> jnp.arange(3)[None, :] & 1
    return (2.0 * corner_bits.astype(jnp.float32) - 1.0) / 4.0


def element_forces(corner_disp, flags, corners):
    gradient = jnp.einsum("eaic,aj->eijc", corner_disp, corners, precision=lax.Precision.HIGHEST)
    strain = 0.5 * (gradient + jnp.swapaxes(gradient, 1, 2))
    volumetric = strain[:, 0, 0] + strain[:, 1, 1] + strain[:, 2, 2]
    identity = jnp.eye(3, dtype=jnp.float32)[None, :, :, None]
    shear_part = 2.0 * SHEAR_MODULUS * (strain - volumetric[:, None, None] / 3.0 * identity)
    magnitude = jnp.sqrt(jnp.sum(shear_part * shear_part, axis=(1, 2)))
    total_modulus = 2.0 * SHEAR_MODULUS + HARDENING
    plastic_factor = HARDENING / total_modulus + 2.0 * SHEAR_MODULUS * YIELD_STRESS / (
        total_modulus * jnp.maximum(magnitude, YIELD_STRESS)
    )
    factor = jnp.where(flags[:, None] == 1, plastic_factor, jnp.ones_like(plastic_factor))
    stress = LAME_FIRST * volumetric[:, None, None] * identity + factor[:, None, None] * shear_part
    return jnp.einsum("eijc,aj->eaic", stress, corners, precision=lax.Precision.HIGHEST)


def apply_scale(values, scales):
    return (values.reshape(scales.shape[0], -1, values.shape[-1]) * scales[:, None, None]).reshape(
        values.shape
    )


def on_device(coef_init, basis, basis_scale, ext_force, precond, connectivity, halo_nodes, plastic):
    rows_dev, cases = ext_force.shape
    node_count = rows_dev // 3
    halo_count = halo_nodes.shape[0]
    corners = corner_table()
    node_ids = jnp.arange(node_count + halo_count, dtype=jnp.int32)
    incidence = (node_ids[:, None] == connectivity.reshape(-1)[None, :]).astype(jnp.float32)
    nodal_residual = ext_force
    coef_out = coef_init
    for sweep in range(ITERS):
        lifted = jnp.dot(
            basis,
            lax.all_gather(coef_out.astype(jnp.bfloat16), "dom", axis=0, tiled=True),
            preferred_element_type=jnp.float32,
        )
        nodes = apply_scale(lifted, basis_scale).reshape(node_count, 3, cases)
        outgoing = nodes[halo_nodes]
        residual_incoming = from_behind(outgoing, "dom", -1)
        extended = jnp.concatenate([nodes, residual_incoming], axis=0)
        corner_force = element_forces(extended[connectivity], plastic, corners)
        internal = jnp.dot(
            incidence,
            corner_force.reshape(-1, 3 * cases),
            precision=lax.Precision.HIGHEST,
            preferred_element_type=jnp.float32,
        ).reshape(node_count + halo_count, 3, cases)
        returned = from_behind(internal[node_count:], "dom", 1)
        own_force = internal[:node_count].at[halo_nodes].add(returned)
        nodal_residual = ext_force - own_force.reshape(rows_dev, cases)
        scaled = apply_scale(nodal_residual, basis_scale).astype(jnp.bfloat16)
        reduced = lax.psum_scatter(
            lax.dot_general(
                basis, scaled, (((0,), (0,)), ((), ())), preferred_element_type=jnp.float32
            ),
            "dom",
            scatter_dimension=0,
            tiled=True,
        )
        update = precond[:, None] * reduced
        squares = lax.psum(jnp.sum(update * update, axis=0), "dom")
        root_mean = jnp.sqrt(squares / R + EPSILON)
        coef_out = coef_out + STEP_SIZE * update / root_mean
    return (coef_out, nodal_residual)


def solution(mesh):
    return jax.shard_map(
        on_device,
        mesh=mesh,
        in_specs=(
            P("dom", None),
            P("dom", None),
            P("dom"),
            P("dom", None),
            P("dom"),
            P("dom", None),
            P("dom"),
            P("dom"),
        ),
        out_specs=(P("dom", None), P("dom", None)),
        check_vma=False,
    )
```

profile of v0, /device:TPU:1, one launch (start us, length us, event | category | flops | bytes accessed | tf_op | source)
XLA Modules:
  0.0 1042.1 jit_solution(15831920046400500216)
XLA Ops:
  9.8 67.0 %all-gather = bf16[256,4,128]{2,1,0:T(4,128)(2,1)S(1)} all-gather(bf16[1,4,128]{2,1,0:T(4,128)(2,1)S(1)} %convert_bitcast_fusion.1), channel_id=1, replica_groups=mesh['dom'=256] {'dom'}, dimensions={0}, use_global_device_ids=true | all-gather | bytes 263168 | tf_op jit(solution)/shard_map/all_gather | solution.py:63
  76.8 1.9 fusion.51
  78.7 2.3 reshape.92
  81.0 2.8 broadcast_multiply_fusion.1
  83.8 3.0 gather_fusion
  86.8 2.1 collective-permute-start
  92.8 4.8 collective-permute-done
  97.6 3.0 pad_maximum_fusion
  100.6 14.1 %gather_fusion.1 = f32[3600,3,128]{2,1,0:T(4,128)} fusion(f32[768,3,128]{2,1,0:T(4,128)} %pad_maximum_fusion, s32[4096]{0:T(1024)S(1)} %pad_clamp_fusion), kind=kCustom, calls=%fused_computation.1 | custom fusion | bytes 11073600 | tf_op jit(solution)/shard_map/gather | solution.py:70
  114.7 8.2 fusion.6
  124.9 2.2 multiply_reduce_fusion.1
  127.3 4.6 multiply_add_fusion.1
  131.8 6.6 convolution_bitcast_fusion.1
  138.4 8.3 fusion.1
  148.5 2.0 copy.43
  150.5 1.9 collective-permute-start.1
  152.5 2.1 slice.67
  154.6 2.5 copy.44
  157.1 1.8 collective-permute-done.1
  158.9 26.5 %scatter_fusion = f32[512,3,128]{2,1,0:T(4,128)} fusion(f32[512,3,128]{2,1,0:T(4,128)} %copy.44, s32[256]{0:T(256)S(1)} %compare_select_fusion.1, f32[256,3,128]{2,1,0:T(4,128)} %collective-permute-done.1), kind=kCustom, calls=%fused_computation.4 | custom fusion | flops 98304 | bytes 1180672 | tf_op jit(solution)/shard_map/scatter-add | solution.py:78
  185.4 2.3 reshape.94
  187.7 3.2 convolution_bitcast_fusion.4
  191.1 253.4 %all-reduce.5.cloned.1.call-done = f32[1024,128]{0,1:T(8,128)} async-done(((f32[1024,128]{0,1:T(8,128)}), f32[1024,128]{0,1:T(8,128)}) %all-reduce.5.cloned.1.call-update) | async-done | bytes 524304
  445.5 77.5 %psum.14 = f32[128]{0:T(128)S(1)} all-reduce(f32[128]{0:T(128)S(1)} %multiply_reduce_fusion.3), channel_id=1, replica_groups=mesh['dom'=256] {'dom'}, use_global_device_ids=true, to_apply=%region_4.5 | all-reduce | flops 128 | bytes 1024 | tf_op jit(solution)/shard_map/psum | solution.py:90
  524.5 58.8 %all-gather.1 = bf16[256,4,128]{2,1,0:T(4,128)(2,1)S(1)} all-gather(bf16[1,4,128]{2,1,0:T(4,128)(2,1)S(1)} %copy.46), channel_id=1, replica_groups=mesh['dom'=256] {'dom'}, dimensions={0}, use_global_device_ids=true | all-gather | bytes 263168 | tf_op jit(solution)/shard_map/all_gather | solution.py:63
  583.4 2.1 convolution_bitcast_fusion.2
  585.4 2.3 copy.47
  587.7 2.3 reshape.95
  590.1 2.8 broadcast_multiply_fusion
  592.9 3.0 gather_fusion.2
  595.9 2.1 collective-permute-start.2
  597.9 8.7 collective-permute-done.2
  606.7 2.8 pad_maximum_fusion.1
  609.5 14.1 %gather_fusion.3 = f32[3600,3,128]{2,1,0:T(4,128)} fusion(f32[768,3,128]{2,1,0:T(4,128)} %pad_maximum_fusion.1, s32[4096]{0:T(1024)S(1)} %pad_clamp_fusion), kind=kCustom, calls=%fused_computation.3 | custom fusion | bytes 11073600 | tf_op jit(solution)/shard_map/gather | solution.py:70
  623.6 8.2 fusion.4
  633.7 2.2 multiply_reduce_fusion
  636.1 4.6 multiply_add_fusion
  640.7 6.6 convolution_bitcast_fusion
  647.3 8.3 fusion
  657.6 1.9 collective-permute-start.3
  659.6 2.1 slice.72
  661.6 2.5 copy.53
  664.1 1.9 collective-permute-done.3
  666.0 26.5 %scatter_fusion.1 = f32[512,3,128]{2,1,0:T(4,128)} fusion(f32[512,3,128]{2,1,0:T(4,128)} %copy.53, s32[256]{0:T(256)S(1)} %compare_select_fusion.1, f32[256,3,128]{2,1,0:T(4,128)} %collective-permute-done.3), kind=kCustom, calls=%fused_computation.5 | custom fusion | flops 98304 | bytes 1180672 | tf_op jit(solution)/shard_map/scatter-add | solution.py:78
  692.5 2.3 reshape.97
  697.1 1.8 convolution_bitcast_fusion.3
  698.9 255.9 %all-reduce.7.cloned.1.call-done = f32[1024,128]{0,1:T(8,128)} async-done(((f32[1024,128]{0,1:T(8,128)}), f32[1024,128]{0,1:T(8,128)}) %all-reduce.7.cloned.1.call-update) | async-done | bytes 524304
  955.8 77.5 %psum.15 = f32[128]{0:T(128)S(1)} all-reduce(f32[128]{0:T(128)S(1)} %multiply_reduce_fusion.2), channel_id=1, replica_groups=mesh['dom'=256] {'dom'}, use_global_device_ids=true, to_apply=%region_9.10 | all-reduce | flops 128 | bytes 1024 | tf_op jit(solution)/shard_map/psum | solution.py:90
  (72 shorter events, 22.2 us)
Async XLA Ops:
  7.2 69.6 %copy-start = (bf16[1536,1024]{1,0:T(8,128)(2,1)S(1)}, bf16[1536,1024]{1,0:T(8,128)(2,1)}, u32[]{:S(2)}) copy-start(bf16[1536,1024]{1,0:T(8,128)(2,1)} %param.9) | copy-start | bytes 9437188
  7.2 437.3 %all-reduce.5.cloned.1.call-start = ((), (), s32[]{:S(2)}) async-start(), calls=%async_computation | async-start | bytes 1048576
  78.7 10.2 copy-start.6
  78.7 14.1 %copy-start.14 = (s32[450]{0:T(512)S(1)}, s32[450]{0:T(512)}, u32[]{:S(2)}) copy-start(s32[450]{0:T(512)} %param.15) | copy-start | bytes 5404
  86.8 10.8 %collective-permute-start = (f32[256,3,128]{2,1,0:T(4,128)}, f32[256,3,128]{2,1,0:T(4,128)}, u32[]{:S(2)}, u32[]{:S(2)}) collective-permute-start(f32[256,3,128]{2,1,0:T(4,128)} %gather_fusion), channel_id=1, source_target_pairs={{1,0},{2,1},{3,2},{4,3},{5,4},{6,5},{7,6},{8,7},{9,8},{10,9},{11,1... | collective-permute-start | bytes 1179656 | tf_op jit(solution)/shard_map/ppermute | solution.py:21
  92.7 45.7 %copy-start.7 = (s32[3600]{0:T(1024)}, s32[3600]{0:T(1024)S(1)}, u32[]{:S(2)}) copy-start(s32[3600]{0:T(1024)S(1)} %eq.35) | copy-start | bytes 43204
  138.4 14.0 %copy-start.13 = (f32[12]{0:T(128)S(1)}, f32[12]{0:T(128)}, u32[]{:S(2)}) copy-start(f32[12]{0:T(128)} %param.10) | copy-start | bytes 148
  146.8 1.0 copy-start.2
  150.5 8.3 collective-permute-start.1
  187.7 3.3 copy-start.10
  187.7 256.8 %copy-start.9 = (f32[4]{0:T(128)S(1)}, f32[4]{0:T(128)}, u32[]{:S(2)}) copy-start(f32[4]{0:T(128)} %param.12) | copy-start | bytes 52
  190.9 763.9 %all-reduce.7.cloned.1.call-start = ((), (), s32[]{:S(2)}) async-start(), calls=%async_computation.1 | async-start | bytes 1048576
  191.0 396.7 %copy-start.4 = (f32[4,128]{0,1:T(8,128)}, f32[4,128]{0,1:T(8,128)S(1)}, u32[]{:S(2)}) copy-start(f32[4,128]{0,1:T(8,128)S(1)} %copy.45) | copy-start | bytes 6148
  523.0 0.5 copy-start.11
  595.9 10.8 %collective-permute-start.2 = (f32[256,3,128]{2,1,0:T(4,128)}, f32[256,3,128]{2,1,0:T(4,128)S(1)}, u32[]{:S(2)}, u32[]{:S(2)}) collective-permute-start(f32[256,3,128]{2,1,0:T(4,128)} %gather_fusion.2), channel_id=1, source_target_pairs={{1,0},{2,1},{3,2},{4,3},{5,4},{6,5},{7,6},{8,7},{9,8},{10,9},{11,1... | collective-permute-start | bytes 1179656 | tf_op jit(solution)/shard_map/ppermute | solution.py:21
  640.7 6.6 copy-start.8
  655.6 1.0 copy-start.3
  657.6 8.3 collective-permute-start.3
  696.2 0.9 copy-start.1
  697.1 336.2 %copy-start.5 = (f32[4,128]{0,1:T(8,128)S(1)}, f32[4,128]{0,1:T(8,128)}, u32[]{:S(2)}) copy-start(f32[4,128]{0,1:T(8,128)} %copy-done.4) | copy-start | bytes 6148
  697.1 336.2 %copy-start.12 = (f32[128]{0:T(128)S(1)}, f32[128]{0:T(128)}, u32[]{:S(2)}) copy-start(f32[128]{0:T(128)} %copy-done.11) | copy-start | bytes 1540
Sparse Core Ops, SparseCore 0:
  191.0 253.4 all-reduce.4
  699.0 255.7 all-reduce.6
where the time goes:
time: 1050 us; the launch traced here: 1040 us
  waiting for transfers between devices  527 us (50%)
  blocking collectives  281 us (27%)
  other arithmetic  89.1 us (8%)
  local copies, waits for them, and re-layouts  67.7 us (6%)
  matrix products  55 us (5%)
  between operations  14.7 us (1%)
    unnamed x4, waiting for transfers between devices  509 us
    psum x2, blocking collectives, on_device(): squares = lax.psum(jnp.sum(update * update, axis=0), 'dom')  155 us
    all_gather x2, blocking collectives, on_device(): lax.all_gather(coef_out.astype(jnp.bfloat16), 'dom', axis=0, tiled=True)  126 us
    scatter-add x2, other arithmetic, on_device(): own_force = internal[:node_count].at[halo_nodes].add(returned)  53 us
    gather x2, local copies, waits for them, and re-layouts, on_device(): corner_force = element_forces(extended[connectivity], plastic, corners)  28.2 us
  transfers between devices with their start and end apart: 6, of which 6 were waited for; matrix products, arithmetic and copies ran while one was open for 1% of the time, Pallas kernels for 0%

commit v1 on v0

v1 whole, which is shorter than its diff:
```python
import functools

import jax
import jax.numpy as jnp
from jax import lax
from jax.experimental import pallas as pl
from jax.experimental.pallas import tpu as pltpu
from jax.sharding import PartitionSpec as P

MESH = pl.DeviceIdType.MESH
F32, BF16 = jnp.float32, jnp.bfloat16

R = 1024
C = 128
ROWS = 1536
LAYER = 256
ELEMS = 450
NDEV = 256
NZ = 8
NQ = 32
BLOCK = 32
CHUNK = 32
STEP_SIZE = 0.5
EPSILON = 1e-05


def dot(a, b):
    return jnp.dot(a, b, preferred_element_type=F32)


def split3(x):
    hi = x.astype(BF16)
    rest = x - hi.astype(F32)
    mid = rest.astype(BF16)
    low = (rest - mid.astype(F32)).astype(BF16)
    return jnp.concatenate([hi, mid, low], axis=1)


def peak(x):
    x = jnp.abs(x)
    for _ in range(x.ndim - 2):
        x = jnp.max(x, axis=0)
    return jnp.maximum(jnp.max(x, axis=0, keepdims=True), 1e-30)


def to_steps(x, top):
    return jnp.round(x * (32767.0 / top)).astype(jnp.int32).astype(jnp.int16)


def from_steps(steps, top):
    return steps.astype(jnp.int32).astype(F32) * (top * (1.0 / 32767.0))


def iota(shape, axis):
    return lax.broadcasted_iota(jnp.int32, shape, axis)


def swap4(x):
    return pltpu.roll(x, 4, x.ndim - 2)


def low_half(shape):
    return iota(shape, len(shape) - 2) % 8 < 4


def kernel(
    coef_ref, scale_ref, precond_ref, conn_ref, halo_ref, plastic_ref, basis_hbm, ext_hbm,
    final_ref, resid_hbm,
    basis, ext, sel, grid_basis, grid_basis_t, scale, grid_ext, resid, out_local, disp, weight, conn,
    tiles, block_init, precond32, gathered, gathered0, coef_low, scaled,
    halo_send, halo_recv, weight_send, weight_recv,
    reduced, part_send, part_recv, zsum_recv, update_recv, square_recv, own_update,
    rest, halo_top, part_top, zsum_top, update_top,
    local_sem, tile_sem, block_sem, halo_sem, weight_sem, part_sem, zsum_sem, update_sem, square_sem, rest_sem,
):
    me = lax.axis_index("dom")
    z, q = me // NQ, me % NQ
    nxt, prv = (me + 1) % NDEV, (me + NDEV - 1) % NDEV

    load_basis = pltpu.make_async_copy(basis_hbm, basis, local_sem.at[0])
    load_ext = pltpu.make_async_copy(ext_hbm, ext, local_sem.at[1])
    load_basis.start()
    load_ext.start()

    def in_plane(j):
        return z * NQ + (q + j) % NQ

    def in_column(j):
        return ((z + j) % NZ) * NQ + q

    barrier = pltpu.get_barrier_semaphore()

    def greet_plane(j, c):
        pl.semaphore_signal(barrier, inc=1, device_id=(in_plane(j),), device_id_type=MESH)
        return c

    def greet_column(j, c):
        pl.semaphore_signal(barrier, inc=1, device_id=(in_column(j),), device_id_type=MESH)
        return c

    lax.fori_loop(1, NQ, greet_plane, 0)
    lax.fori_loop(1, NZ, greet_column, 0)
    pl.semaphore_signal(barrier, inc=1, device_id=(nxt,), device_id_type=MESH)
    pl.semaphore_signal(barrier, inc=1, device_id=(prv,), device_id_type=MESH)

    tiles[z, 0:4, :] = coef_ref[...]
    row4 = iota((4, C), 0)
    pre = jnp.zeros((4, C), F32)
    for k in range(4):
        pre = jnp.where(row4 == k, precond_ref[k], pre)
    tiles[z, 4:8, :] = pre

    pl.semaphore_wait(barrier, NQ - 1 + NZ - 1 + 2)

    def send_column(src, buf, sems):
        def body(j, c):
            pltpu.make_async_remote_copy(
                src, buf.at[z], sems.at[0], sems.at[1], device_id=(in_column(j),), device_id_type=MESH
            ).start()
            return c

        lax.fori_loop(1, NZ, body, 0)

    def send_plane(src_of, buf, sems):
        def body(j, c):
            pltpu.make_async_remote_copy(
                src_of((q + j) % NQ), buf.at[q], sems.at[0], sems.at[1], device_id=(in_plane(j),), device_id_type=MESH
            ).start()
            return c

        lax.fori_loop(1, NQ, body, 0)

    def wait_for(buf, count, sem):
        part = buf.at[pl.ds(0, count)]
        pltpu.make_async_copy(part, part, sem).wait()

    send_column(tiles.at[z], tiles, tile_sem)

    conn[...] = jnp.full(conn.shape, -1.0, F32)
    conn[0:8, 0:ELEMS] = conn_ref[...].astype(F32)
    conn[8:9, 0:ELEMS] = plastic_ref[...].astype(F32)
    halo_row = halo_ref[...].astype(F32)
    eye = iota((LAYER, LAYER), 0) == iota((LAYER, LAYER), 1)
    node0 = jnp.sum(jnp.where(eye, halo_row, 0.0), axis=1, keepdims=True)
    place = iota((LAYER, 512), 0).astype(F32) + 512.0
    found = jnp.full((LAYER, 512), -1.0, F32)
    for a in range(4):
        found = jnp.maximum(found, jnp.where(conn[4 + a : 5 + a, :] == place, conn[a : a + 1, :], -1.0))
    node1 = jnp.max(found, axis=1, keepdims=True)
    flags = conn[8:9, :]
    flag1 = jnp.sum(jnp.where(conn[0:1, :] == node0, flags, 0.0), axis=1, keepdims=True)
    flag2 = jnp.sum(jnp.where(conn[4:5, :] == place, flags, 0.0), axis=1, keepdims=True)
    cell = iota((LAYER, C), 0)
    valid = (cell % 16 < 15) & (cell // 16 < 15)
    weight[1] = jnp.where(valid, 1.0 + flag1, 0.0)
    weight[2] = jnp.where(valid, 1.0 + flag2, 0.0)
    weight_send[...] = weight[2].astype(BF16)
    to_next = pltpu.make_async_remote_copy(
        weight_send, weight_recv, weight_sem.at[0], weight_sem.at[1], device_id=(nxt,), device_id_type=MESH
    )
    to_next.start()

    column = iota((LAYER, ROWS), 1)
    for layer, node in enumerate((node0, node1)):
        node3 = node.astype(jnp.int32) * 3
        for i in range(3):
            at = (layer * 3 + i) * LAYER
            sel[at : at + LAYER, :] = jnp.where(column == node3 + i, 1.0, 0.0).astype(BF16)
            tile = jnp.broadcast_to((node3 + i) >> 7, (LAYER, C))
            value = jnp.zeros((LAYER, C), F32)
            for t in range(12):
                value = jnp.where(tile == t, scale_ref[t], value)
            scale[at : at + LAYER, :] = value

    wait_for(tiles, NZ - 1, tile_sem.at[1])
    low = low_half((8, C))
    for j in range(4):
        a, b = tiles[2 * j], tiles[2 * j + 1]
        block_init[8 * j : 8 * j + 8, :] = jnp.where(low, a, swap4(b))
        precond32[8 * j : 8 * j + 8, :] = jnp.where(low, swap4(a), b)
    first = block_init[...].astype(BF16)
    gathered[q] = first
    send_plane(lambda _: gathered.at[q], gathered, block_sem)
    rest[q] = (block_init[...] - first.astype(F32)).astype(BF16)
    send_plane(lambda _: rest.at[q], rest, rest_sem)

    load_basis.wait()

    def permute(c, carry):
        rows = pl.ds(pl.multiple_of(c * LAYER, LAYER), LAYER)
        grid_basis[rows, :] = dot(sel[rows, :], basis[...]).astype(BF16)
        return carry

    lax.fori_loop(0, 6, permute, 0)

    zero_rows = jnp.zeros((16, C), F32)
    for k in range(12):
        disp[k, LAYER : LAYER + 16, :] = zero_rows
    for k in range(6):
        resid[k, LAYER : LAYER + 16, :] = zero_rows

    def place_rows(values):
        v = values.reshape(16, 2, 4, 8, C)
        first, second = v[:, 0], v[:, 1]
        mask = low_half((16, 4, 8, C))
        even = jnp.where(mask, first, swap4(second))
        odd = jnp.where(mask, swap4(first), second)
        for j in range(4):
            coef_low[256 * j : 256 * j + 128, :] = even[:, j].reshape(128, C).astype(BF16)
            coef_low[256 * j + 128 : 256 * j + 256, :] = odd[:, j].reshape(128, C).astype(BF16)

    wait_for(gathered, NQ - 1, block_sem.at[1])
    place_rows(gathered[...].astype(F32))

    def elements(k):
        def body(c, carry):
            at = pl.multiple_of(c * CHUNK, CHUNK)
            node_rows = pl.ds(at, CHUNK + 16)
            n = CHUNK + 16
            grad = []
            for i in range(3):
                under, over = disp[3 * k + i, node_rows, :], disp[3 * k + 3 + i, node_rows, :]
                under1, over1 = pltpu.roll(under, n - 1, 0), pltpu.roll(over, n - 1, 0)
                both, both1 = under + over, under1 + over1
                dx = both1 - both
                sx = both1 + both
                sz = (over1 + over) - (under1 + under)
                grad.append((dx[16:] + dx[:CHUNK], sx[16:] - sx[:CHUNK], sz[16:] + sz[:CHUNK]))
            w = weight[k, pl.ds(at, CHUNK), :]
            third = (grad[0][0] + grad[1][1] + grad[2][2]) * (1.0 / 6.0)
            sxx = grad[0][0] * 0.5 - third
            syy = grad[1][1] * 0.5 - third
            szz = grad[2][2] * 0.5 - third
            sxy = (grad[0][1] + grad[1][0]) * 0.25
            sxz = (grad[0][2] + grad[2][0]) * 0.25
            syz = (grad[1][2] + grad[2][1]) * 0.25
            mag2 = sxx * sxx + syy * syy + szz * szz + 2.0 * (sxy * sxy + sxz * sxz + syz * syz)
            plastic = 0.05 + 0.6 * lax.rsqrt(jnp.maximum(mag2, 9.0))
            factor = jnp.where(w > 1.5, plastic, jnp.where(w > 0.5, 0.25, 0.0))
            vol = jnp.where(w > 0.5, third * 0.5625, 0.0)
            stress = {
                (0, 0): vol + factor * sxx, (1, 1): vol + factor * syy, (2, 2): vol + factor * szz,
                (0, 1): factor * sxy, (0, 2): factor * sxz, (1, 2): factor * syz,
            }
            back = {ij: pltpu.roll(s, 1, 0) for ij, s in stress.items()}
            pad = jnp.zeros((16, C), F32)
            for i in range(3):
                ix, iy, iz = (0, i), (min(i, 1), max(i, 1)), (i, 2)
                dx = back[ix] - stress[ix]
                sy = back[iy] + stress[iy]
                sz = back[iz] + stress[iz]
                near, far = dx - sy, dx + sy
                if k >= 1:
                    rows = (3 * (k - 1) + i, node_rows, slice(None))
                    resid[rows] -= jnp.concatenate([near - sz, pad], 0) + jnp.concatenate([pad, far - sz], 0)
                if k <= 1:
                    rows = (3 * k + i, node_rows, slice(None))
                    resid[rows] -= jnp.concatenate([near + sz, pad], 0) + jnp.concatenate([pad, far + sz], 0)
            return carry

        lax.fori_loop(0, LAYER // CHUNK, body, 0)

    for sweep in range(2):
        def displace(c, carry):
            rows = pl.ds(pl.multiple_of(c * LAYER, LAYER), LAYER)
            u = dot(grid_basis[rows, :], coef_low[...]) * scale[rows, :]
            disp[c + 3, 0:LAYER, :] = u
            return carry

        copies = []
        for layer, (there, side) in enumerate(((prv, 1), (nxt, 0))):
            lax.fori_loop(3 * layer, 3 * layer + 3, displace, 0)
            u = disp[3 + 3 * layer : 6 + 3 * layer, 0:LAYER, :]
            top = peak(u)
            halo_top[sweep, layer] = top
            halo_send[sweep, layer] = to_steps(u, top)
            for src, dst, sem in (
                (halo_send.at[sweep, layer], halo_recv.at[sweep, side], 0),
                (halo_top.at[sweep, layer], halo_top.at[sweep, 2 + side], 1),
            ):
                copy = pltpu.make_async_remote_copy(
                    src, dst, halo_sem.at[sweep, layer, sem, 0], halo_sem.at[sweep, layer, sem, 1],
                    device_id=(there,), device_id_type=MESH,
                )
                copy.start()
                copies.append(copy)

        if sweep == 0:
            load_ext.wait()
            ext3 = split3(ext[...])

            def permute_ext(c, carry):
                rows = pl.ds(pl.multiple_of(c * LAYER, LAYER), LAYER)
                e = dot(sel[rows, :], ext3)
                grid_ext[c] = e[:, 0:C] + e[:, C : 2 * C] + e[:, 2 * C :]
                return carry

            lax.fori_loop(0, 6, permute_ext, 0)

            def turn(c, carry):
                rows = pl.ds(pl.multiple_of(c * LAYER, LAYER), LAYER)
                for b in range(4):
                    grid_basis_t[b * 256 : b * 256 + 256, rows] = grid_basis[rows, b * 256 : b * 256 + 256].T
                return carry

            lax.fori_loop(0, 6, turn, 0)
            to_next.wait()
            weight[0] = jnp.where(me > 0, weight_recv[...].astype(F32), 0.0)

        resid[:, 0:LAYER, :] = grid_ext[...]
        elements(1)
        for copy in copies:
            copy.wait()
        disp[0:3, 0:LAYER, :] = from_steps(halo_recv[sweep, 0], halo_top[sweep, 2][None])
        disp[9:12, 0:LAYER, :] = jnp.where(
            me < NDEV - 1, from_steps(halo_recv[sweep, 1], halo_top[sweep, 3][None]), 0.0
        )
        elements(0)
        elements(2)
        for k in range(6):
            rows = slice(k * LAYER, (k + 1) * LAYER)
            scaled[rows, :] = (resid[k, 0:LAYER, :] * scale[rows, :]).astype(BF16)

        def project(j, carry):
            rows = pl.ds(pl.multiple_of(j * 256, 256), 256)
            r = dot(grid_basis_t[rows, :], scaled[...]).reshape(2, 16, 8, C)
            even, odd = r[0], r[1]
            mask = low_half((16, 8, C))
            at = pl.ds(pl.multiple_of(j * 8, 8), 8)
            reduced[:, 0, at, :] = jnp.where(mask, even, swap4(odd))
            reduced[:, 1, at, :] = jnp.where(mask, swap4(even), odd)
            return carry

        lax.fori_loop(0, 4, project, 0)
        parts = reduced[...].reshape(NQ, BLOCK, C)
        top = peak(parts)
        part_top[sweep, q] = top
        send_plane(lambda _: part_top.at[sweep, q], part_top.at[sweep], part_sem.at[sweep, 1])
        part_send[sweep] = to_steps(parts, top[None])
        part_recv[sweep, q] = part_send[sweep, q]
        send_plane(lambda t: part_send.at[sweep, t], part_recv.at[sweep], part_sem.at[sweep, 0])

        if sweep == 1:
            out_local[...] = jnp.zeros_like(out_local)

            def restore(c, carry):
                rows = pl.ds(pl.multiple_of(c * LAYER, LAYER), LAYER)
                o = lax.dot_general(
                    sel[rows, :], split3(resid[c, 0:LAYER, :]), (((0,), (0,)), ((), ())), preferred_element_type=F32
                )
                out_local[...] += o[:, 0:C] + o[:, C : 2 * C] + o[:, 2 * C :]
                return carry

            lax.fori_loop(0, 6, restore, 0)
            store = pltpu.make_async_copy(out_local, resid_hbm, local_sem.at[2])
            store.start()

        wait_for(part_top.at[sweep], NQ - 1, part_sem.at[sweep, 1, 1])
        wait_for(part_recv.at[sweep], NQ - 1, part_sem.at[sweep, 0, 1])
        total = from_steps(part_recv[sweep, 0], part_top[sweep, 0])
        for t in range(1, NQ):
            total += from_steps(part_recv[sweep, t], part_top[sweep, t])
        top = peak(total)
        zsum_top[sweep, z] = top
        send_column(zsum_top.at[sweep, z], zsum_top.at[sweep], zsum_sem.at[sweep, 1])
        zsum_recv[sweep, z] = to_steps(total, top)
        send_column(zsum_recv.at[sweep, z], zsum_recv.at[sweep], zsum_sem.at[sweep, 0])
        wait_for(zsum_top.at[sweep], NZ - 1, zsum_sem.at[sweep, 1, 1])
        wait_for(zsum_recv.at[sweep], NZ - 1, zsum_sem.at[sweep, 0, 1])
        total = from_steps(zsum_recv[sweep, 0], zsum_top[sweep, 0])
        for t in range(1, NZ):
            total += from_steps(zsum_recv[sweep, t], zsum_top[sweep, t])
        update = total * precond32[...]

        if sweep == 0:
            own_update[...] = update
            top = peak(update)
            update_top[q] = top
            send_plane(lambda _: update_top.at[q], update_top, update_sem.at[1])
            update_recv[q] = to_steps(update, top)
            send_plane(lambda _: update_recv.at[q], update_recv, update_sem.at[0])
            wait_for(rest, NQ - 1, rest_sem.at[1])
            gathered0[...] = gathered[...].astype(F32) + rest[...].astype(F32)
            wait_for(update_top, NQ - 1, update_sem.at[1, 1])
            wait_for(update_recv, NQ - 1, update_sem.at[0, 1])
            u = from_steps(update_recv[...], update_top[...])
            squares = jnp.sum(u * u, axis=(0, 1), keepdims=False)[None, :]
            inverse = STEP_SIZE * lax.rsqrt(squares * (1.0 / R) + EPSILON)
            place_rows(gathered0[...] + u * inverse[None])
            block_init[...] += own_update[...] * inverse
        else:
            square_recv[q] = jnp.sum(update * update, axis=0, keepdims=True)
            send_plane(lambda _: square_recv.at[q], square_recv, square_sem)
            wait_for(square_recv, NQ - 1, square_sem.at[1])
            squares = jnp.sum(square_recv[...], axis=0)
            inverse = STEP_SIZE * lax.rsqrt(squares * (1.0 / R) + EPSILON)
            final = block_init[...] + update * inverse
            mine = jnp.zeros((8, C), F32)
            for j in range(4):
                mine = jnp.where(z // 2 == j, final[8 * j : 8 * j + 8], mine)
            mine = jnp.where(z % 2 == 0, mine, swap4(mine))
            final_ref[...] = mine[0:4]

    wait_for(tiles, NZ - 1, tile_sem.at[0])
    wait_for(gathered, NQ - 1, block_sem.at[0])
    wait_for(rest, NQ - 1, rest_sem.at[0])
    wait_for(update_recv, NQ - 1, update_sem.at[0, 0])
    wait_for(update_top, NQ - 1, update_sem.at[1, 0])
    wait_for(square_recv, NQ - 1, square_sem.at[0])
    for sweep in range(2):
        wait_for(part_recv.at[sweep], NQ - 1, part_sem.at[sweep, 0, 0])
        wait_for(part_top.at[sweep], NQ - 1, part_sem.at[sweep, 1, 0])
        wait_for(zsum_recv.at[sweep], NZ - 1, zsum_sem.at[sweep, 0, 0])
        wait_for(zsum_top.at[sweep], NZ - 1, zsum_sem.at[sweep, 1, 0])
    store.wait()


def on_device(coef_init, basis, basis_scale, ext_force, precond, connectivity, halo_nodes, plastic):
    vmem = pl.BlockSpec(memory_space=pltpu.VMEM)
    smem = pl.BlockSpec(memory_space=pltpu.SMEM)
    anywhere = pl.BlockSpec(memory_space=pl.ANY)
    dma = pltpu.SemaphoreType.DMA
    return pl.pallas_call(
        kernel,
        out_shape=(jax.ShapeDtypeStruct((4, C), F32), jax.ShapeDtypeStruct((ROWS, C), F32)),
        in_specs=[vmem, smem, smem, vmem, vmem, vmem, anywhere, anywhere],
        out_specs=(vmem, anywhere),
        scratch_shapes=[
            pltpu.VMEM((ROWS, R), BF16),
            pltpu.VMEM((ROWS, C), F32),
            pltpu.VMEM((ROWS, ROWS), BF16),
            pltpu.VMEM((ROWS, R), BF16),
            pltpu.VMEM((R, ROWS), BF16),
            pltpu.VMEM((ROWS, C), F32),
            pltpu.VMEM((6, LAYER, C), F32),
            pltpu.VMEM((6, LAYER + 16, C), F32),
            pltpu.VMEM((ROWS, C), F32),
            pltpu.VMEM((12, LAYER + 16, C), F32),
            pltpu.VMEM((3, LAYER, C), F32),
            pltpu.VMEM((16, 512), F32),
            pltpu.VMEM((NZ, 8, C), F32),
            pltpu.VMEM((BLOCK, C), F32),
            pltpu.VMEM((BLOCK, C), F32),
            pltpu.VMEM((NQ, BLOCK, C), BF16),
            pltpu.VMEM((NQ, BLOCK, C), F32),
            pltpu.VMEM((R, C), BF16),
            pltpu.VMEM((ROWS, C), BF16),
            pltpu.VMEM((2, 2, 3, LAYER, C), jnp.int16),
            pltpu.VMEM((2, 2, 3, LAYER, C), jnp.int16),
            pltpu.VMEM((LAYER, C), BF16),
            pltpu.VMEM((LAYER, C), BF16),
            pltpu.VMEM((16, 2, BLOCK, C), F32),
            pltpu.VMEM((2, NQ, BLOCK, C), jnp.int16),
            pltpu.VMEM((2, NQ, BLOCK, C), jnp.int16),
            pltpu.VMEM((2, NZ, BLOCK, C), jnp.int16),
            pltpu.VMEM((NQ, BLOCK, C), jnp.int16),
            pltpu.VMEM((NQ, 1, C), F32),
            pltpu.VMEM((BLOCK, C), F32),
            pltpu.VMEM((NQ, BLOCK, C), BF16),
            pltpu.VMEM((2, 4, 1, C), F32),
            pltpu.VMEM((2, NQ, 1, C), F32),
            pltpu.VMEM((2, NZ, 1, C), F32),
            pltpu.VMEM((NQ, 1, C), F32),
            dma((3,)),
            dma((2,)),
            dma((2,)),
            dma((2, 2, 2, 2)),
            dma((2,)),
            dma((2, 2, 2)),
            dma((2, 2, 2)),
            dma((2, 2)),
            dma((2,)),
            dma((2,)),
        ],
        compiler_params=pltpu.CompilerParams(
            collective_id=0, has_side_effects=True, vmem_limit_bytes=56 << 20
        ),
        cost_estimate=pl.CostEstimate(flops=14_000_000_000, bytes_accessed=6_000_000, transcendentals=0),
        name="galerkin",
    )(
        coef_init, basis_scale, precond, connectivity.T, halo_nodes.reshape(1, LAYER), plastic.reshape(1, ELEMS),
        basis, ext_force,
    )


def solution(mesh):
    return jax.shard_map(
        on_device,
        mesh=mesh,
        in_specs=(
            P("dom", None), P("dom", None), P("dom"), P("dom", None), P("dom"), P("dom", None), P("dom"), P("dom"),
        ),
        out_specs=(P("dom", None), P("dom", None)),
        check_vma=False,
    )
```

time: 1050 us -> 85 us (0.08)
  waiting for transfers between devices: 527 us -> 0 us
  blocking collectives: 281 us -> 0 us
  other arithmetic: 89.1 us -> 0 us
  Pallas kernels: 0 us -> 80.9 us
  local copies, waits for them, and re-layouts: 67.7 us -> 3.32 us
  matrix products: 55 us -> 0 us
  between operations: 14.7 us -> 0.64 us
    unnamed x4 -> x0, waiting for transfers between devices: 509 us -> none
    psum x2 -> x0, blocking collectives: 155 us -> none  [on_device(): squares = lax.psum(jnp.sum(update * update, axis=0), 'dom')]
    all_gather x2 -> x0, blocking collectives: 126 us -> none  [on_device(): lax.all_gather(coef_out.astype(jnp.bfloat16), 'dom', axis=0, tiled=True)]
    pallas_call x0 -> x1, Pallas kernels: none -> 80.9 us  [on_device(): pl.pallas_call(kernel, out_shape=(jax.ShapeDtypeStruct((4, C), F32), jax....]
    dot_general x10 -> x0, matrix products: 55 us -> none  [the longest x2 16.6 us: on_device(): jnp.dot(incidence, corner_force.reshape(-1, 3 * cases), precision=lax.Pre...]
    scatter-add x2 -> x0, other arithmetic: 53 us -> none  [on_device(): own_force = internal[:node_count].at[halo_nodes].add(returned)]
    gather x4 -> x0, local copies, waits for them, and re-layouts: 34.2 us -> none  [the longest x2 28.2 us: on_device(): corner_force = element_forces(extended[connectivity], plastic, corners)]
    ppermute x4 -> x0, waiting for transfers between devices: 17.3 us -> none  [from_behind(): lax.ppermute(value, axis, [(source, source + steps) for source in range(l...]
  transfers between devices with their start and end apart: 6 -> 0, of which waited for: 6 -> 0; matrix products, arithmetic and copies ran while one was open for 1% -> 0% of each run, Pallas kernels for 0% -> 0%
where the time goes in v1:
time: 85 us; the launch traced here: 84.8 us
  Pallas kernels  80.9 us (95%)
  local copies, waits for them, and re-layouts  3.32 us (4%)
    pallas_call x1, Pallas kernels, on_device(): pl.pallas_call(kernel, out_shape=(jax.ShapeDtypeStruct((4, C), F32), jax....  80.9 us
    unnamed x2, local copies, waits for them, and re-layouts  3.32 us

profile of v1, /device:TPU:1, one launch (start us, length us, event | category | flops | bytes accessed | tf_op | source)
XLA Modules:
  0.0 84.8 jit_solution(8452185703355240918)
XLA Ops:
  0.6 80.9 %galerkin.1 = (f32[4,128]{1,0:T(4,128)}, f32[1536,128]{1,0:T(8,128)}) custom-call(f32[4,128]{1,0:T(4,128)} %coef_ref.1, f32[12]{0:T(128)} %scale_ref.1, f32[4]{0:T(128)} %precond_ref.1, s32[8,450]{1,0:T(8,128)} %bitcast.3, s32[1,256]{1,0:T(1,128)} %bitcast.5, s32[1,450]{1,0:T(1,128)} %bitcast.4, bf16[1536,1024]{1,0:T(8,128)(2,1)} %basis_hbm.1, ...), custom_call_target="tpu_custom_call" | custom-call | flops 14000000000 | bytes 6000000 | tf_op jit(solution)/shard_map/galerkin/pallas_call | solution.py:423
  81.5 1.3 %copy.12 = f32[4,128]{1,0:T(4,128)} copy(f32[4,128]{1,0:T(4,128)} %get-tuple-element.4) | data formatting | bytes 4096
  82.8 2.1 %copy.13 = f32[1536,128]{1,0:T(8,128)} copy(f32[1536,128]{1,0:T(8,128)} %get-tuple-element.5) | data formatting | bytes 1572864

commit v2 on v1

--- a/solution.py
+++ b/solution.py
@@ -65,8 +65,8 @@
 
 def kernel(
     coef_ref, scale_ref, precond_ref, conn_ref, halo_ref, plastic_ref, basis_hbm, ext_hbm,
-    final_ref, resid_hbm,
-    basis, ext, sel, grid_basis, grid_basis_t, scale, grid_ext, resid, out_local, disp, weight, conn,
+    final_ref, out_local,
+    basis, ext, sel, grid_basis, grid_basis_t, scale, grid_ext, resid, disp, weight, conn, nodes,
     tiles, block_init, precond32, gathered, gathered0, coef_low, scaled,
     halo_send, halo_recv, weight_send, weight_recv,
     reduced, part_send, part_recv, zsum_recv, update_recv, square_recv, own_update,
@@ -112,7 +112,11 @@
 
     pl.semaphore_wait(barrier, NQ - 1 + NZ - 1 + 2)
 
+    pending = []
+
     def send_column(src, buf, sems):
+        pending.append((buf, NZ - 1, sems.at[0]))
+
         def body(j, c):
             pltpu.make_async_remote_copy(
                 src, buf.at[z], sems.at[0], sems.at[1], device_id=(in_column(j),), device_id_type=MESH
@@ -122,6 +126,8 @@
         lax.fori_loop(1, NZ, body, 0)
 
     def send_plane(src_of, buf, sems):
+        pending.append((buf, NQ - 1, sems.at[0]))
+
         def body(j, c):
             pltpu.make_async_remote_copy(
                 src_of((q + j) % NQ), buf.at[q], sems.at[0], sems.at[1], device_id=(in_plane(j),), device_id_type=MESH
@@ -140,37 +146,49 @@
     conn[0:8, 0:ELEMS] = conn_ref[...].astype(F32)
     conn[8:9, 0:ELEMS] = plastic_ref[...].astype(F32)
     halo_row = halo_ref[...].astype(F32)
-    eye = iota((LAYER, LAYER), 0) == iota((LAYER, LAYER), 1)
-    node0 = jnp.sum(jnp.where(eye, halo_row, 0.0), axis=1, keepdims=True)
-    place = iota((LAYER, 512), 0).astype(F32) + 512.0
-    found = jnp.full((LAYER, 512), -1.0, F32)
-    for a in range(4):
-        found = jnp.maximum(found, jnp.where(conn[4 + a : 5 + a, :] == place, conn[a : a + 1, :], -1.0))
-    node1 = jnp.max(found, axis=1, keepdims=True)
-    flags = conn[8:9, :]
-    flag1 = jnp.sum(jnp.where(conn[0:1, :] == node0, flags, 0.0), axis=1, keepdims=True)
-    flag2 = jnp.sum(jnp.where(conn[4:5, :] == place, flags, 0.0), axis=1, keepdims=True)
-    cell = iota((LAYER, C), 0)
-    valid = (cell % 16 < 15) & (cell // 16 < 15)
-    weight[1] = jnp.where(valid, 1.0 + flag1, 0.0)
-    weight[2] = jnp.where(valid, 1.0 + flag2, 0.0)
-    weight_send[...] = weight[2].astype(BF16)
+
+    def decode(c, carry):
+        at = pl.multiple_of(c * 32, 32)
+        rows = pl.ds(at, 32)
+        place = (iota((32, 512), 0) + (at + 512)).astype(F32)
+        found = jnp.full((32, 512), -1.0, F32)
+        for a in range(4):
+            found = jnp.maximum(found, jnp.where(conn[4 + a : 5 + a, :] == place, conn[a : a + 1, :], -1.0))
+        node1 = jnp.max(found, axis=1, keepdims=True)
+        mine = iota((32, LAYER), 0) + at == iota((32, LAYER), 1)
+        node0 = jnp.sum(jnp.where(mine, halo_row, 0.0), axis=1, keepdims=True)
+        flags = conn[8:9, :]
+        flag1 = jnp.sum(jnp.where(conn[0:1, :] == node0, flags, 0.0), axis=1, keepdims=True)
+        flag2 = jnp.sum(jnp.where(conn[4:5, :] == place, flags, 0.0), axis=1, keepdims=True)
+        cell = iota((32, C), 0) + at
+        valid = (cell % 16 < 15) & (cell // 16 < 15)
+        weight[1, rows, :] = jnp.where(valid, 1.0 + flag1, 0.0)
+        second = jnp.where(valid, 1.0 + flag2, 0.0)
+        weight[2, rows, :] = second
+        weight_send[rows, :] = second.astype(BF16)
+        nodes[rows, :] = jnp.broadcast_to(node0 * 3.0, (32, C)).astype(jnp.int32)
+        nodes[pl.ds(pl.multiple_of(LAYER + c * 32, 32), 32), :] = jnp.broadcast_to(node1 * 3.0, (32, C)).astype(jnp.int32)
+        return carry
+
+    lax.fori_loop(0, LAYER // 32, decode, 0)
+
     to_next = pltpu.make_async_remote_copy(
         weight_send, weight_recv, weight_sem.at[0], weight_sem.at[1], device_id=(nxt,), device_id_type=MESH
     )
     to_next.start()
 
-    column = iota((LAYER, ROWS), 1)
-    for layer, node in enumerate((node0, node1)):
-        node3 = node.astype(jnp.int32) * 3
+    lane = iota((16, C), 1)
+
+    def select(c, carry):
+        node3 = nodes[pl.ds(pl.multiple_of(c * 16, 16), 16), :]
         for i in range(3):
-            at = (layer * 3 + i) * LAYER
-            sel[at : at + LAYER, :] = jnp.where(column == node3 + i, 1.0, 0.0).astype(BF16)
-            tile = jnp.broadcast_to((node3 + i) >> 7, (LAYER, C))
-            value = jnp.zeros((LAYER, C), F32)
-            for t in range(12):
-                value = jnp.where(tile == t, scale_ref[t], value)
-            scale[at : at + LAYER, :] = value
+            rows = pl.ds(pl.multiple_of((c // 16 * 3 + i) * LAYER + c % 16 * 16, 16), 16)
+            away = node3 + i - lane
+            for t in range(ROWS // C):
+                sel[rows, C * t : C * t + C] = jnp.where(away == C * t, 1.0, 0.0).astype(BF16)
+        return carry
+
+    lax.fori_loop(0, 32, select, 0)
 
     wait_for(tiles, NZ - 1, tile_sem.at[1])
     low = low_half((8, C))
@@ -187,11 +205,23 @@
     load_basis.wait()
 
     def permute(c, carry):
-        rows = pl.ds(pl.multiple_of(c * LAYER, LAYER), LAYER)
+        rows = pl.ds(pl.multiple_of(c * 768, 768), 768)
         grid_basis[rows, :] = dot(sel[rows, :], basis[...]).astype(BF16)
         return carry
 
-    lax.fori_loop(0, 6, permute, 0)
+    lax.fori_loop(0, 2, permute, 0)
+
+    def scales(c, carry):
+        node3 = nodes[pl.ds(pl.multiple_of(c * 16, 16), 16), :]
+        for i in range(3):
+            tile = (node3 + i) >> 7
+            value = jnp.zeros((16, C), F32)
+            for t in range(12):
+                value = jnp.where(tile == t, scale_ref[t], value)
+            scale[pl.ds(pl.multiple_of((c // 16 * 3 + i) * LAYER + c % 16 * 16, 16), 16), :] = value
+        return carry
+
+    lax.fori_loop(0, 32, scales, 0)
 
     zero_rows = jnp.zeros((16, C), F32)
     for k in range(12):
@@ -261,17 +291,15 @@
         lax.fori_loop(0, LAYER // CHUNK, body, 0)
 
     for sweep in range(2):
-        def displace(c, carry):
-            rows = pl.ds(pl.multiple_of(c * LAYER, LAYER), LAYER)
-            u = dot(grid_basis[rows, :], coef_low[...]) * scale[rows, :]
-            disp[c + 3, 0:LAYER, :] = u
-            return carry
-
         copies = []
         for layer, (there, side) in enumerate(((prv, 1), (nxt, 0))):
-            lax.fori_loop(3 * layer, 3 * layer + 3, displace, 0)
+            top = jnp.full((1, C), 1e-30, F32)
+            for i in range(3):
+                rows = slice((3 * layer + i) * LAYER, (3 * layer + i + 1) * LAYER)
+                u = dot(grid_basis[rows, :], coef_low[...]) * scale[rows, :]
+                disp[3 + 3 * layer + i, 0:LAYER, :] = u
+                top = jnp.maximum(top, peak(u))
             u = disp[3 + 3 * layer : 6 + 3 * layer, 0:LAYER, :]
-            top = peak(u)
             halo_top[sweep, layer] = top
             halo_send[sweep, layer] = to_steps(u, top)
             for src, dst, sem in (
@@ -321,24 +349,19 @@
             rows = slice(k * LAYER, (k + 1) * LAYER)
             scaled[rows, :] = (resid[k, 0:LAYER, :] * scale[rows, :]).astype(BF16)
 
-        def project(j, carry):
-            rows = pl.ds(pl.multiple_of(j * 256, 256), 256)
-            r = dot(grid_basis_t[rows, :], scaled[...]).reshape(2, 16, 8, C)
+        mask = low_half((16, 8, C))
+        for j in range(4):
+            r = dot(grid_basis_t[256 * j : 256 * j + 256, :], scaled[...]).reshape(2, 16, 8, C)
             even, odd = r[0], r[1]
-            mask = low_half((16, 8, C))
-            at = pl.ds(pl.multiple_of(j * 8, 8), 8)
-            reduced[:, 0, at, :] = jnp.where(mask, even, swap4(odd))
-            reduced[:, 1, at, :] = jnp.where(mask, swap4(even), odd)
-            return carry
-
-        lax.fori_loop(0, 4, project, 0)
+            reduced[:, 0, 8 * j : 8 * j + 8, :] = jnp.where(mask, even, swap4(odd))
+            reduced[:, 1, 8 * j : 8 * j + 8, :] = jnp.where(mask, swap4(even), odd)
         parts = reduced[...].reshape(NQ, BLOCK, C)
         top = peak(parts)
         part_top[sweep, q] = top
-        send_plane(lambda _: part_top.at[sweep, q], part_top.at[sweep], part_sem.at[sweep, 1])
         part_send[sweep] = to_steps(parts, top[None])
         part_recv[sweep, q] = part_send[sweep, q]
         send_plane(lambda t: part_send.at[sweep, t], part_recv.at[sweep], part_sem.at[sweep, 0])
+        send_plane(lambda _: part_top.at[sweep, q], part_top.at[sweep], part_sem.at[sweep, 1])
 
         if sweep == 1:
             out_local[...] = jnp.zeros_like(out_local)
@@ -352,19 +375,17 @@
                 return carry
 
             lax.fori_loop(0, 6, restore, 0)
-            store = pltpu.make_async_copy(out_local, resid_hbm, local_sem.at[2])
-            store.start()
-
+
+        wait_for(part_recv.at[sweep], NQ - 1, part_sem.at[sweep, 0, 1])
         wait_for(part_top.at[sweep], NQ - 1, part_sem.at[sweep, 1, 1])
-        wait_for(part_recv.at[sweep], NQ - 1, part_sem.at[sweep, 0, 1])
         total = from_steps(part_recv[sweep, 0], part_top[sweep, 0])
         for t in range(1, NQ):
             total += from_steps(part_recv[sweep, t], part_top[sweep, t])
         top = peak(total)
         zsum_top[sweep, z] = top
-        send_column(zsum_top.at[sweep, z], zsum_top.at[sweep], zsum_sem.at[sweep, 1])
         zsum_recv[sweep, z] = to_steps(total, top)
         send_column(zsum_recv.at[sweep, z], zsum_recv.at[sweep], zsum_sem.at[sweep, 0])
+        send_column(zsum_top.at[sweep, z], zsum_top.at[sweep], zsum_sem.at[sweep, 1])
         wait_for(zsum_top.at[sweep], NZ - 1, zsum_sem.at[sweep, 1, 1])
         wait_for(zsum_recv.at[sweep], NZ - 1, zsum_sem.at[sweep, 0, 1])
         total = from_steps(zsum_recv[sweep, 0], zsum_top[sweep, 0])
@@ -376,9 +397,9 @@
             own_update[...] = update
             top = peak(update)
             update_top[q] = top
-            send_plane(lambda _: update_top.at[q], update_top, update_sem.at[1])
             update_recv[q] = to_steps(update, top)
             send_plane(lambda _: update_recv.at[q], update_recv, update_sem.at[0])
+            send_plane(lambda _: update_top.at[q], update_top, update_sem.at[1])
             wait_for(rest, NQ - 1, rest_sem.at[1])
             gathered0[...] = gathered[...].astype(F32) + rest[...].astype(F32)
             wait_for(update_top, NQ - 1, update_sem.at[1, 1])
@@ -401,18 +422,8 @@
             mine = jnp.where(z % 2 == 0, mine, swap4(mine))
             final_ref[...] = mine[0:4]
 
-    wait_for(tiles, NZ - 1, tile_sem.at[0])
-    wait_for(gathered, NQ - 1, block_sem.at[0])
-    wait_for(rest, NQ - 1, rest_sem.at[0])
-    wait_for(update_recv, NQ - 1, update_sem.at[0, 0])
-    wait_for(update_top, NQ - 1, update_sem.at[1, 0])
-    wait_for(square_recv, NQ - 1, square_sem.at[0])
-    for sweep in range(2):
-        wait_for(part_recv.at[sweep], NQ - 1, part_sem.at[sweep, 0, 0])
-        wait_for(part_top.at[sweep], NQ - 1, part_sem.at[sweep, 1, 0])
-        wait_for(zsum_recv.at[sweep], NZ - 1, zsum_sem.at[sweep, 0, 0])
-        wait_for(zsum_top.at[sweep], NZ - 1, zsum_sem.at[sweep, 1, 0])
-    store.wait()
+    for sent in pending:
+        wait_for(*sent)
 
 
 def on_device(coef_init, basis, basis_scale, ext_force, precond, connectivity, halo_nodes, plastic):
@@ -422,9 +433,9 @@
     dma = pltpu.SemaphoreType.DMA
     return pl.pallas_call(
         kernel,
-        out_shape=(jax.ShapeDtypeStruct((4, C), F32), jax.ShapeDtypeStruct((ROWS, C), F32)),
+        out_shape=(pltpu.VMEM((4, C), F32), pltpu.VMEM((ROWS, C), F32)),
         in_specs=[vmem, smem, smem, vmem, vmem, vmem, anywhere, anywhere],
-        out_specs=(vmem, anywhere),
+        out_specs=(vmem, vmem),
         scratch_shapes=[
             pltpu.VMEM((ROWS, R), BF16),
             pltpu.VMEM((ROWS, C), F32),
@@ -434,10 +445,10 @@
             pltpu.VMEM((ROWS, C), F32),
             pltpu.VMEM((6, LAYER, C), F32),
             pltpu.VMEM((6, LAYER + 16, C), F32),
-            pltpu.VMEM((ROWS, C), F32),
             pltpu.VMEM((12, LAYER + 16, C), F32),
             pltpu.VMEM((3, LAYER, C), F32),
             pltpu.VMEM((16, 512), F32),
+            pltpu.VMEM((2 * LAYER, C), jnp.int32),
             pltpu.VMEM((NZ, 8, C), F32),
             pltpu.VMEM((BLOCK, C), F32),
             pltpu.VMEM((BLOCK, C), F32),
@@ -461,7 +472,7 @@
             pltpu.VMEM((2, NQ, 1, C), F32),
             pltpu.VMEM((2, NZ, 1, C), F32),
             pltpu.VMEM((NQ, 1, C), F32),
-            dma((3,)),
+            dma((2,)),
             dma((2,)),
             dma((2,)),
             dma((2, 2, 2, 2)),
@@ -473,7 +484,7 @@
             dma((2,)),
         ],
         compiler_params=pltpu.CompilerParams(
-            collective_id=0, has_side_effects=True, vmem_limit_bytes=56 << 20
+            collective_id=0, has_side_effects=True, vmem_limit_bytes=58 << 20
         ),
         cost_estimate=pl.CostEstimate(flops=14_000_000_000, bytes_accessed=6_000_000, transcendentals=0),
         name="galerkin",

time: 85 us -> 81.3 us (0.956)
  local copies, waits for them, and re-layouts: 3.32 us -> 1.46 us
  Pallas kernels: 80.9 us -> 79.1 us
    unnamed x2, local copies, waits for them, and re-layouts: 3.32 us -> 1.46 us
    pallas_call x1, Pallas kernels: 80.9 us -> 79.1 us  [on_device(): pl.pallas_call(kernel, out_shape=(pltpu.VMEM((4, C), F32), pltpu.VMEM((RO...]
where the time goes in v2:
time: 81.3 us; the launch traced here: 81.2 us
  Pallas kernels  79.1 us (97%)
  local copies, waits for them, and re-layouts  1.46 us (2%)
    pallas_call x1, Pallas kernels, on_device(): pl.pallas_call(kernel, out_shape=(pltpu.VMEM((4, C), F32), pltpu.VMEM((RO...  79.1 us

profile of v2, /device:TPU:1, one launch (start us, length us, event | category | flops | bytes accessed | tf_op | source)
XLA Modules:
  0.0 81.2 jit_solution(15404843907562861003)
XLA Ops:
  0.6 79.1 %galerkin.1 = (f32[4,128]{1,0:T(4,128)S(1)}, f32[1536,128]{1,0:T(8,128)S(1)}) custom-call(f32[4,128]{1,0:T(4,128)} %coef_ref.1, f32[12]{0:T(128)} %scale_ref.1, f32[4]{0:T(128)} %precond_ref.1, s32[8,450]{1,0:T(8,128)} %bitcast.3, s32[1,256]{1,0:T(1,128)} %bitcast.5, s32[1,450]{1,0:T(1,128)} %bitcast.4, bf16[1536,1024]{1,0:T(8,128)(2,1)} %basis_hbm.1, ...), custom_call_target="tpu_custom_call" | custom-call | flops 14000000000 | bytes 6000000 | tf_op jit(solution)/shard_map/galerkin/pallas_call | solution.py:434
  79.8 0.6 copy.12
  80.3 0.9 %copy.13 = f32[1536,128]{1,0:T(8,128)} copy(f32[1536,128]{1,0:T(8,128)S(1)} %get-tuple-element.3) | data formatting | bytes 1572864

commit v3 on v2

--- a/solution.py
+++ b/solution.py
@@ -290,28 +290,27 @@
 
         lax.fori_loop(0, LAYER // CHUNK, body, 0)
 
+    sent_pieces = []
     for sweep in range(2):
-        copies = []
-        for layer, (there, side) in enumerate(((prv, 1), (nxt, 0))):
-            top = jnp.full((1, C), 1e-30, F32)
-            for i in range(3):
+        pieces = ([], [])
+        for i in range(3):
+            for layer, (there, side) in enumerate(((prv, 1), (nxt, 0))):
                 rows = slice((3 * layer + i) * LAYER, (3 * layer + i + 1) * LAYER)
                 u = dot(grid_basis[rows, :], coef_low[...]) * scale[rows, :]
                 disp[3 + 3 * layer + i, 0:LAYER, :] = u
-                top = jnp.maximum(top, peak(u))
-            u = disp[3 + 3 * layer : 6 + 3 * layer, 0:LAYER, :]
-            halo_top[sweep, layer] = top
-            halo_send[sweep, layer] = to_steps(u, top)
-            for src, dst, sem in (
-                (halo_send.at[sweep, layer], halo_recv.at[sweep, side], 0),
-                (halo_top.at[sweep, layer], halo_top.at[sweep, 2 + side], 1),
-            ):
-                copy = pltpu.make_async_remote_copy(
-                    src, dst, halo_sem.at[sweep, layer, sem, 0], halo_sem.at[sweep, layer, sem, 1],
-                    device_id=(there,), device_id_type=MESH,
-                )
-                copy.start()
-                copies.append(copy)
+                top = peak(u)
+                halo_top[sweep, layer, i] = top
+                halo_send[sweep, layer, i] = to_steps(u, top)
+                for src, dst, kind in (
+                    (halo_send.at[sweep, layer, i], halo_recv.at[sweep, side, i], 0),
+                    (halo_top.at[sweep, layer, i], halo_top.at[sweep, 2 + side, i], 1),
+                ):
+                    sems = halo_sem.at[sweep, 6 * layer + 2 * i + kind]
+                    copy = pltpu.make_async_remote_copy(
+                        src, dst, sems.at[0], sems.at[1], device_id=(there,), device_id_type=MESH
+                    )
+                    copy.start()
+                    pieces[layer].append(copy)
 
         if sweep == 0:
             load_ext.wait()
@@ -337,14 +336,14 @@
 
         resid[:, 0:LAYER, :] = grid_ext[...]
         elements(1)
-        for copy in copies:
-            copy.wait()
-        disp[0:3, 0:LAYER, :] = from_steps(halo_recv[sweep, 0], halo_top[sweep, 2][None])
-        disp[9:12, 0:LAYER, :] = jnp.where(
-            me < NDEV - 1, from_steps(halo_recv[sweep, 1], halo_top[sweep, 3][None]), 0.0
-        )
-        elements(0)
-        elements(2)
+        for layer, side in ((0, 1), (1, 0)):
+            for copy in pieces[layer]:
+                copy.wait_recv()
+            for i in range(3):
+                u = from_steps(halo_recv[sweep, side, i], halo_top[sweep, 2 + side, i])
+                disp[9 * side + i, 0:LAYER, :] = jnp.where(me < NDEV - 1, u, 0.0) if side == 1 else u
+            elements(2 * side)
+        sent_pieces += pieces[0] + pieces[1]
         for k in range(6):
             rows = slice(k * LAYER, (k + 1) * LAYER)
             scaled[rows, :] = (resid[k, 0:LAYER, :] * scale[rows, :]).astype(BF16)
@@ -422,6 +421,8 @@
             mine = jnp.where(z % 2 == 0, mine, swap4(mine))
             final_ref[...] = mine[0:4]
 
+    for copy in sent_pieces:
+        copy.wait_send()
     for sent in pending:
         wait_for(*sent)
 
@@ -468,14 +469,14 @@
             pltpu.VMEM((NQ, 1, C), F32),
             pltpu.VMEM((BLOCK, C), F32),
             pltpu.VMEM((NQ, BLOCK, C), BF16),
-            pltpu.VMEM((2, 4, 1, C), F32),
+            pltpu.VMEM((2, 4, 3, 1, C), F32),
             pltpu.VMEM((2, NQ, 1, C), F32),
             pltpu.VMEM((2, NZ, 1, C), F32),
             pltpu.VMEM((NQ, 1, C), F32),
             dma((2,)),
             dma((2,)),
             dma((2,)),
-            dma((2, 2, 2, 2)),
+            dma((2, 12, 2)),
             dma((2,)),
             dma((2, 2, 2)),
             dma((2, 2, 2)),

time: 81.3 us -> 80.1 us (0.985)
  Pallas kernels: 79.1 us -> 77.8 us
    pallas_call x1, Pallas kernels: 79.1 us -> 77.8 us  [on_device(): pl.pallas_call(kernel, out_shape=(pltpu.VMEM((4, C), F32), pltpu.VMEM((RO...]
where the time goes in v3:
time: 80.1 us; the launch traced here: 79.9 us
  Pallas kernels  77.8 us (97%)
  local copies, waits for them, and re-layouts  1.46 us (2%)
    pallas_call x1, Pallas kernels, on_device(): pl.pallas_call(kernel, out_shape=(pltpu.VMEM((4, C), F32), pltpu.VMEM((RO...  77.8 us

profile of v3, /device:TPU:1, one launch (start us, length us, event | category | flops | bytes accessed | tf_op | source)
XLA Modules:
  0.0 79.9 jit_solution(6381454900365696133)
XLA Ops:
  0.6 77.8 %galerkin.1 = (f32[4,128]{1,0:T(4,128)S(1)}, f32[1536,128]{1,0:T(8,128)S(1)}) custom-call(f32[4,128]{1,0:T(4,128)} %coef_ref.1, f32[12]{0:T(128)} %scale_ref.1, f32[4]{0:T(128)} %precond_ref.1, s32[8,450]{1,0:T(8,128)} %bitcast.3, s32[1,256]{1,0:T(1,128)} %bitcast.5, s32[1,450]{1,0:T(1,128)} %bitcast.4, bf16[1536,1024]{1,0:T(8,128)(2,1)} %basis_hbm.1, ...), custom_call_target="tpu_custom_call" | custom-call | flops 14000000000 | bytes 6000000 | tf_op jit(solution)/shard_map/galerkin/pallas_call | solution.py:435
  78.5 0.6 copy.12
  79.1 0.9 %copy.13 = f32[1536,128]{1,0:T(8,128)} copy(f32[1536,128]{1,0:T(8,128)S(1)} %get-tuple-element.3) | data formatting | bytes 1572864

commit v4 on v3

--- a/solution.py
+++ b/solution.py
@@ -19,7 +19,7 @@
 NZ = 8
 NQ = 32
 BLOCK = 32
-CHUNK = 32
+CHUNK = 64
 STEP_SIZE = 0.5
 EPSILON = 1e-05
 

time: 80.1 us -> 79.8 us (level)
  no operation moved by 1% of the time
where the time goes in v4:
time: 79.8 us; the launch traced here: 79.7 us
  Pallas kernels  77.6 us (97%)
  local copies, waits for them, and re-layouts  1.46 us (2%)
    pallas_call x1, Pallas kernels, on_device(): pl.pallas_call(kernel, out_shape=(pltpu.VMEM((4, C), F32), pltpu.VMEM((RO...  77.6 us

profile of v4, /device:TPU:1, one launch (start us, length us, event | category | flops | bytes accessed | tf_op | source)
XLA Modules:
  0.0 79.7 jit_solution(7135302966629450865)
XLA Ops:
  0.6 77.6 %galerkin.1 = (f32[4,128]{1,0:T(4,128)S(1)}, f32[1536,128]{1,0:T(8,128)S(1)}) custom-call(f32[4,128]{1,0:T(4,128)} %coef_ref.1, f32[12]{0:T(128)} %scale_ref.1, f32[4]{0:T(128)} %precond_ref.1, s32[8,450]{1,0:T(8,128)} %bitcast.3, s32[1,256]{1,0:T(1,128)} %bitcast.5, s32[1,450]{1,0:T(1,128)} %bitcast.4, bf16[1536,1024]{1,0:T(8,128)(2,1)} %basis_hbm.1, ...), custom_call_target="tpu_custom_call" | custom-call | flops 14000000000 | bytes 6000000 | tf_op jit(solution)/shard_map/galerkin/pallas_call | solution.py:435
  78.2 0.6 copy.12
  78.8 0.9 %copy.13 = f32[1536,128]{1,0:T(8,128)} copy(f32[1536,128]{1,0:T(8,128)S(1)} %get-tuple-element.3) | data formatting | bytes 1572864
